TPU v7x, 32 devices: a whole 2x2x4 slice. The times are simulated.
32 devices in a mesh: seq: 16 (over z, y, x), ffn: 2 (over core).
Axes of the slice: x: 2, y: 2, z: 4, core: 2. Of those that a mesh axis runs over, the one named last changes fastest.
Arguments:
- x_long: bfloat16 [2, 4096, 768], P(None, ('seq', 'ffn')), may hold values from -6 to 6
- x_glob: bfloat16 [2, 64, 768], P(None, ('seq', 'ffn')), may hold values from -6 to 6
- sentence: int32 [2, 16, 256], P(None, 'seq'), may hold values from 0 to 3, never falling along the last dimension, each value on 1 to 96 neighbouring positions
- dy_long: bfloat16 [2, 4096, 768], P(None, ('seq', 'ffn')), may hold values from -6 to 6
- dy_glob: bfloat16 [2, 64, 768], P(None, ('seq', 'ffn')), may hold values from -6 to 6
- owner_list: int32 [224], replicated, may hold values from 0 to 223, as said below
- w_master: float32 [448, 128, 128], P(('seq', 'ffn')), may hold values from -0.57735027 to 0.57735027
- m_old: float32 [448, 128, 128], P(('seq', 'ffn')), may hold values from -20.249516 to 20.249516
- v_old: float32 [448, 128, 128], P(('seq', 'ffn')), may hold values from 4.37632 to 437.632, as said below
- left_basis: float32 [448, 128, 128], P(('seq', 'ffn')), may hold values from -1 to 1, as said below
- right_basis: float32 [448, 128, 128], P(('seq', 'ffn')), may hold values from -1 to 1, as said below
- left_stats: float32 [448, 128, 128], P(('seq', 'ffn')), may hold values from 0 to 1064960, as said below
- right_stats: float32 [448, 128, 128], P(('seq', 'ffn')), may hold values from 0 to 1064960, as said below
- rel_table: float32 [169, 768], P(None, 'ffn'), may hold values from -6 to 6
- rel_m: float32 [169, 768], P(None, 'ffn'), may hold values from -3 to 3
- rel_v: float32 [169, 768], P(None, 'ffn'), may hold values from 0.17472 to 0.69888
- norm_params: float32 [4, 768], replicated, may hold values from -0.8 to 1.3
- norm_m: float32 [4, 768], replicated, may hold values from -64 to 64
- norm_v: float32 [4, 768], replicated, may hold values from 437.632 to 1747.2
Outputs:
- y_long: bfloat16 [2, 4096, 768], P(None, ('seq', 'ffn'))
- y_glob: bfloat16 [2, 64, 768], P(None, ('seq', 'ffn'))
- dx_long: float32 [2, 4096, 768], P(None, ('seq', 'ffn'))
- dx_glob: float32 [2, 64, 768], P(None, ('seq', 'ffn'))
- w_new: float32 [448, 128, 128], P(('seq', 'ffn'))
- m_new: float32 [448, 128, 128], P(('seq', 'ffn'))
- v_new: float32 [448, 128, 128], P(('seq', 'ffn'))
- left_basis_new: float32 [448, 128, 128], P(('seq', 'ffn'))
- right_basis_new: float32 [448, 128, 128], P(('seq', 'ffn'))
- left_stats_new: float32 [448, 128, 128], P(('seq', 'ffn'))
- right_stats_new: float32 [448, 128, 128], P(('seq', 'ffn'))
- rel_new: float32 [169, 768], P(None, 'ffn')
- rel_m_new: float32 [169, 768], P(None, 'ffn')
- rel_v_new: float32 [169, 768], P(None, 'ffn')
- norm_new: float32 [4, 768], replicated
- norm_m_new: float32 [4, 768], replicated
- norm_v_new: float32 [4, 768], replicated
Inputs may be any that keep to these rules, and one draw needn't show every extreme that they name: For each sequence s and block b, sentence[s, b, t] never falls along t, every value is used, and no value covers more than 96 tokens. `owner_list`: all entries differ. `v_old`: positive. `left_basis`: each slot's matrix is orthogonal. `right_basis`: each slot's matrix is orthogonal. `left_stats`: each slot's matrix is diagonal with a positive diagonal. `right_stats`: each slot's matrix is diagonal with a positive diagonal.
All inputs are finite; a program needn't handle non-finite values.
Results may differ from a plain program's by a relative error of at most 0.015.
The roundings to bfloat16 on the way count: a program that leaves them out, or rounds other values in their place, can miss the bound.
Values may be sent and summed in bfloat16 or wider, within the bound.
No kernel may reach another device: no remote copies, remote signals or barrier semaphores. Data moves between devices by JAX's collectives and lax.ppermute only.
A program may use at most 192 MiB of HBM per device.

v0:
```python
import math

import jax
import jax.numpy as jnp
from jax import lax
from jax.sharding import PartitionSpec as P

HEADS = 12
FF = 3072
RADIUS = 84
STEP = 10


BETA_ONE = 0.9
BETA_TWO = 0.95
LEARN_RATE = 0.02
ADAM_RATE = 0.6
WEIGHT_DECAY = 0.01
ADAM_EPS = 1e-08
NORM_EPS = 1e-12
NEG_FILL = -1e30
TOP_PRECISION = lax.Precision.HIGHEST


def with_halo(cells, sides, width):
    for axis, dim in sides:
        count = lax.axis_size(axis)
        ends = count - 1
        head = lax.slice_in_dim(cells, 0, width, axis=dim)
        tail = lax.slice_in_dim(cells, cells.shape[dim] - width, cells.shape[dim], axis=dim)
        cells = jnp.concatenate(
            [
                lax.ppermute(tail, axis, [(i, (i + 1) % count) for i in range(ends)]),
                cells,
                lax.ppermute(head, axis, [((i + 1) % count, i) for i in range(ends)]),
            ],
            axis=dim,
        )
    return cells


def assemble(tile_set, row_count, col_count):
    side_len = tile_set.shape[-1]
    tile_grid = tile_set.reshape(row_count // side_len, col_count // side_len, side_len, side_len)
    return tile_grid.transpose(0, 2, 1, 3).reshape(row_count, col_count)


def cut_tiles(matrix, side_len):
    row_count, col_count = matrix.shape
    tile_grid = matrix.reshape(row_count // side_len, side_len, col_count // side_len, side_len)
    return tile_grid.transpose(0, 2, 1, 3).reshape(-1, side_len, side_len)


def skew_rows(label_table, span_len):
    lead_dims = label_table.shape[:-2]
    row_count, labels = (label_table.shape[-2], label_table.shape[-1])
    padded = jnp.pad(label_table, [(0, 0)] * len(lead_dims) + [(0, 0), (0, span_len + 1 - labels)])
    flat_rows = padded.reshape(lead_dims + (row_count * (span_len + 1),))
    return flat_rows[..., : row_count * span_len].reshape(lead_dims + (row_count, span_len))


def unskew_rows(score_grid, labels):
    lead_dims = score_grid.shape[:-2]
    row_count, span_len = (score_grid.shape[-2], score_grid.shape[-1])
    padded = jnp.pad(score_grid, [(0, 0)] * len(lead_dims) + [(0, 0), (0, 1)])
    flat_rows = padded.reshape(lead_dims + (row_count * (span_len + 1),))
    flat_rows = jnp.pad(flat_rows, [(0, 0)] * len(lead_dims) + [(0, row_count)])
    return flat_rows.reshape(lead_dims + (row_count, span_len + 2))[..., :labels]


def layer_norm(values, gain_vec, offset):
    center = values - jnp.mean(values, axis=-1, keepdims=True)
    spread = jnp.mean(center * center, axis=-1, keepdims=True)
    return center * lax.rsqrt(spread + NORM_EPS) * gain_vec + offset


def gelu_tanh(values):
    return jax.nn.gelu(values, approximate=True)


def log_total(first_part, second_part):
    top_val = jnp.maximum(jnp.max(first_part, axis=-1), jnp.max(second_part, axis=-1))
    total_sum = jnp.sum(jnp.exp(first_part - top_val[..., None]), axis=-1) + jnp.sum(
        jnp.exp(second_part - top_val[..., None]), axis=-1
    )
    return top_val + jnp.log(total_sum)


def scores_of(queries, keys_in):
    return jnp.einsum("gihe,gkhe->ghik", queries, keys_in, preferred_element_type=jnp.float32)


def weigh_values(weights, values):
    return jnp.einsum("ghik,gkhe->gihe", weights, values, preferred_element_type=jnp.float32)


def key_grad(score_grads, queries, scale):
    return (
        jnp.einsum("ghik,gihe->gkhe", score_grads, queries, preferred_element_type=jnp.float32)
        * scale
    )


def long_scores(q_long, k_ext, k_all, rel_heads, window_mask, scale):
    near_scores = scores_of(q_long, k_ext)
    rel_part = jnp.einsum("gihe,lhe->ghil", q_long, rel_heads, preferred_element_type=jnp.float32)
    near_scores = jnp.where(
        window_mask, (near_scores + skew_rows(rel_part, k_ext.shape[1])) * scale, NEG_FILL
    )
    return (near_scores, scores_of(q_long, k_all) * scale)


def glob_scores(q_glob, k_loc, k_all, sent_mask, scale):
    own_scores = jnp.where(sent_mask, scores_of(q_glob, k_loc) * scale, NEG_FILL)
    return (own_scores, scores_of(q_glob, k_all) * scale)


def part_back(first_part, second_part, lse_rows, grad_out, v_first, v_second):
    p_first = jnp.exp(first_part - lse_rows[..., None])
    p_second = jnp.exp(second_part - lse_rows[..., None])
    dp_first = scores_of(grad_out, v_first)
    dp_second = scores_of(grad_out, v_second)
    row_delta = jnp.sum(p_first * dp_first, axis=-1) + jnp.sum(p_second * dp_second, axis=-1)
    ds_first = (p_first * (dp_first - row_delta[..., None])).astype(jnp.bfloat16)
    ds_second = (p_second * (dp_second - row_delta[..., None])).astype(jnp.bfloat16)
    dv_first = jnp.einsum(
        "ghik,gihe->gkhe",
        p_first.astype(jnp.bfloat16),
        grad_out,
        preferred_element_type=jnp.float32,
    )
    dv_second = jnp.einsum(
        "ghik,gihe->gkhe",
        p_second.astype(jnp.bfloat16),
        grad_out,
        preferred_element_type=jnp.float32,
    )
    return (ds_first, ds_second, dv_first, dv_second)


def einsum_high(formula, *operands):
    return jnp.einsum(formula, *operands, precision=TOP_PRECISION)


def sandwich(left_q, middle, right_q):
    return einsum_high("nik,nkl->nil", einsum_high("nji,njk->nik", left_q, middle), right_q)


def chol_orth(matrix):
    gram_mat = einsum_high("nji,njk->nik", matrix, matrix)
    lower_f = jnp.linalg.cholesky(gram_mat)
    solved = lax.linalg.triangular_solve(
        lower_f, jnp.swapaxes(matrix, 1, 2), left_side=True, lower=True
    )
    return jnp.swapaxes(solved, 1, 2)


def soap_update(grad_tile, weight, first_mom, second_mom, left_q, right_q, left_s, right_s):
    rotated = sandwich(left_q, grad_tile, right_q)
    first_mom = BETA_ONE * first_mom + (1.0 - BETA_ONE) * rotated
    second_mom = BETA_TWO * second_mom + (1.0 - BETA_TWO) * rotated * rotated
    direction = (
        first_mom
        / (1.0 - BETA_ONE**STEP)
        / (jnp.sqrt(second_mom / (1.0 - BETA_TWO**STEP)) + ADAM_EPS)
    )
    back_rot = einsum_high("nik,nlk->nil", einsum_high("nij,njk->nik", left_q, direction), right_q)
    weight = weight - LEARN_RATE * (back_rot + WEIGHT_DECAY * weight)
    left_s = BETA_TWO * left_s + (1.0 - BETA_TWO) * einsum_high(
        "nik,njk->nij", grad_tile, grad_tile
    )
    right_s = BETA_TWO * right_s + (1.0 - BETA_TWO) * einsum_high(
        "nki,nkj->nij", grad_tile, grad_tile
    )
    left_q = chol_orth(einsum_high("nij,njk->nik", left_s, left_q))
    right_q = chol_orth(einsum_high("nij,njk->nik", right_s, right_q))
    return (weight, first_mom, second_mom, left_q, right_q, left_s, right_s)


def adam_update(grad_vals, param, first_mom, second_mom, decay_rate):
    first_mom = BETA_ONE * first_mom + (1.0 - BETA_ONE) * grad_vals
    second_mom = BETA_TWO * second_mom + (1.0 - BETA_TWO) * grad_vals * grad_vals
    direction = (
        first_mom
        / (1.0 - BETA_ONE**STEP)
        / (jnp.sqrt(second_mom / (1.0 - BETA_TWO**STEP)) + ADAM_EPS)
    )
    return (param - ADAM_RATE * (direction + decay_rate * param), first_mom, second_mom)


def on_device(
    x_long,
    x_glob,
    sentence,
    dy_long,
    dy_glob,
    owner_list,
    w_master,
    m_old,
    v_old,
    left_basis,
    right_basis,
    left_stats,
    right_stats,
    rel_table,
    rel_m,
    rel_v,
    norm_params,
    norm_m,
    norm_v,
):
    ffn_count = lax.axis_size("ffn")
    seq_count = lax.axis_size("seq")
    seq_total, tok_half, model_dim = x_long.shape
    glob_half = x_glob.shape[1]
    block_len = tok_half * ffn_count
    glob_block = glob_half * ffn_count
    head_local = model_dim // ffn_count
    hidden_local = FF // ffn_count
    heads_here = HEADS // ffn_count
    head_size = model_dim // HEADS
    score_scale = head_size ** (-0.5)
    side_len = w_master.shape[1]
    attn_tiles = model_dim * head_local // (side_len * side_len)
    ffn_tiles = model_dim * hidden_local // (side_len * side_len)
    tile_count = 4 * attn_tiles + 2 * ffn_tiles
    slot_count = owner_list.shape[0]
    owner_used = owner_list[:tile_count]
    labels = rel_table.shape[0]
    span_len = block_len + 2 * RADIUS
    group_len = math.gcd(seq_total, 4)
    half_index = lax.axis_index("ffn")
    gathered = lax.all_gather(w_master.astype(jnp.bfloat16), "seq", axis=0, tiled=True)
    tile_set = jnp.take(gathered, owner_used, axis=0)
    w_qkv = jnp.concatenate(
        [
            assemble(
                tile_set[part_idx * attn_tiles : (part_idx + 1) * attn_tiles], model_dim, head_local
            )
            for part_idx in range(3)
        ],
        axis=1,
    )
    w_out = assemble(tile_set[3 * attn_tiles : 4 * attn_tiles], head_local, model_dim)
    w_up = assemble(tile_set[4 * attn_tiles : 4 * attn_tiles + ffn_tiles], model_dim, hidden_local)
    w_down = assemble(tile_set[4 * attn_tiles + ffn_tiles : tile_count], hidden_local, model_dim)
    rel_heads = rel_table.astype(jnp.bfloat16).reshape(labels, heads_here, head_size)
    start_pos = lax.axis_index("seq") * block_len
    key_pos = start_pos - RADIUS + jnp.arange(span_len, dtype=jnp.int32)
    offsets = (
        jnp.arange(span_len, dtype=jnp.int32)[None, :]
        - jnp.arange(block_len, dtype=jnp.int32)[:, None]
    )
    window_mask = (
        (offsets >= 0)
        & (offsets <= 2 * RADIUS)
        & (key_pos >= 0)[None, :]
        & (key_pos < block_len * seq_count)[None, :]
    )[None, None]
    sent_mask = (
        sentence[:, 0][:, None, :] == jnp.arange(glob_block, dtype=jnp.int32)[None, :, None]
    )[:, None]

    def split_heads(values):
        return values.reshape(values.shape[:-1] + (heads_here, head_size))

    def merge_heads(values):
        return values.reshape(values.shape[:-2] + (head_local,))

    def grouped(values):
        return values.reshape((seq_total // group_len, group_len) + values.shape[1:])

    def ungrouped(values):
        return values.reshape((seq_total,) + values.shape[2:])

    def project_keys(rows_in):
        proj_rows = jnp.einsum(
            "snd,dc->snc", rows_in, w_qkv, preferred_element_type=jnp.float32
        ).astype(jnp.bfloat16)
        key_ext = with_halo(proj_rows[:, :block_len, head_local:], (("seq", 1),), RADIUS)
        glob_kv = lax.all_gather(proj_rows[:, block_len:, head_local:], "seq", axis=1, tiled=True)
        return (proj_rows, key_ext, glob_kv)

    def attention_inputs(proj_rows, key_ext, glob_kv):
        return (
            split_heads(proj_rows[:, :block_len, :head_local]),
            split_heads(proj_rows[:, block_len:, :head_local]),
            split_heads(key_ext[..., :head_local]),
            split_heads(key_ext[..., head_local:]),
            split_heads(glob_kv[..., :head_local]),
            split_heads(glob_kv[..., head_local:]),
        )

    def attend_group(pieces):
        q_long, q_glob, k_ext, v_ext, k_all, v_all, sent_grp = pieces
        k_loc = k_ext[:, RADIUS : RADIUS + block_len]
        v_loc = v_ext[:, RADIUS : RADIUS + block_len]
        near_scores, far_scores = long_scores(
            q_long, k_ext, k_all, rel_heads, window_mask, score_scale
        )
        lse_long = log_total(near_scores, far_scores)
        out_long = weigh_values(
            jnp.exp(near_scores - lse_long[..., None]).astype(jnp.bfloat16), v_ext
        ) + weigh_values(jnp.exp(far_scores - lse_long[..., None]).astype(jnp.bfloat16), v_all)
        own_scores, glob_far = glob_scores(q_glob, k_loc, k_all, sent_grp, score_scale)
        lse_glob = log_total(own_scores, glob_far)
        out_glob = weigh_values(
            jnp.exp(own_scores - lse_glob[..., None]).astype(jnp.bfloat16), v_loc
        ) + weigh_values(jnp.exp(glob_far - lse_glob[..., None]).astype(jnp.bfloat16), v_all)
        return (out_long.astype(jnp.bfloat16), out_glob.astype(jnp.bfloat16), lse_long, lse_glob)

    def attend_back(pieces):
        (
            q_long,
            q_glob,
            k_ext,
            v_ext,
            k_all,
            v_all,
            sent_grp,
            lse_long,
            lse_glob,
            do_long,
            do_glob,
        ) = pieces
        k_loc = k_ext[:, RADIUS : RADIUS + block_len]
        v_loc = v_ext[:, RADIUS : RADIUS + block_len]
        near_scores, far_scores = long_scores(
            q_long, k_ext, k_all, rel_heads, window_mask, score_scale
        )
        ds_near, ds_far, dv_ext, dv_all = part_back(
            near_scores, far_scores, lse_long, do_long, v_ext, v_all
        )
        rel_rows = unskew_rows(ds_near, labels)
        dq_long = (
            weigh_values(ds_near, k_ext)
            + weigh_values(ds_far, k_all)
            + jnp.einsum("ghil,lhe->gihe", rel_rows, rel_heads, preferred_element_type=jnp.float32)
        ) * score_scale
        d_rel = (
            jnp.einsum("ghil,gihe->lhe", rel_rows, q_long, preferred_element_type=jnp.float32)
            * score_scale
        )
        dk_ext = key_grad(ds_near, q_long, score_scale)
        dk_all = key_grad(ds_far, q_long, score_scale)
        own_scores, glob_far = glob_scores(q_glob, k_loc, k_all, sent_grp, score_scale)
        ds_own, ds_gfar, dv_loc, dv_gall = part_back(
            own_scores, glob_far, lse_glob, do_glob, v_loc, v_all
        )
        dq_glob = (weigh_values(ds_own, k_loc) + weigh_values(ds_gfar, k_all)) * score_scale
        dk_loc = key_grad(ds_own, q_glob, score_scale)
        dk_all = dk_all + key_grad(ds_gfar, q_glob, score_scale)
        dv_all = dv_all + dv_gall
        return (dq_long, dq_glob, dk_ext, dv_ext, dk_loc, dv_loc, dk_all, dv_all, d_rel)

    long_rows, glob_rows = (
        lax.all_gather(x_long, "ffn", axis=1, tiled=True),
        lax.all_gather(x_glob, "ffn", axis=1, tiled=True),
    )
    all_rows = jnp.concatenate([long_rows, glob_rows], axis=1)
    proj_rows, key_ext, glob_kv = project_keys(all_rows)
    att_in = attention_inputs(proj_rows, key_ext, glob_kv)
    fwd_out = lax.map(attend_group, tuple((grouped(member) for member in att_in + (sent_mask,))))
    out_long, out_glob, lse_long, lse_glob = tuple((ungrouped(member) for member in fwd_out))
    out_rows = jnp.concatenate([merge_heads(out_long), merge_heads(out_glob)], axis=1)
    attn_part = jnp.einsum("snc,cd->snd", out_rows, w_out, preferred_element_type=jnp.float32)
    attn_full = lax.psum(attn_part, "ffn")
    mid_rows = all_rows.astype(jnp.float32) + attn_full
    norm_one = layer_norm(mid_rows, norm_params[0], norm_params[1])
    norm_low = norm_one.astype(jnp.bfloat16)
    up_pre = jnp.einsum("snd,df->snf", norm_low, w_up, preferred_element_type=jnp.float32)
    act_low = gelu_tanh(up_pre).astype(jnp.bfloat16)
    down_part = jnp.einsum("snf,fd->snd", act_low, w_down, preferred_element_type=jnp.float32)
    gelu_val, gelu_back = jax.vjp(gelu_tanh, up_pre)
    down_full = lax.psum(down_part, "ffn")
    pre_out = norm_one + down_full
    layer_out = layer_norm(pre_out, norm_params[2], norm_params[3])
    y_long = lax.dynamic_slice_in_dim(
        layer_out[:, :block_len], half_index * tok_half, tok_half, 1
    ).astype(jnp.bfloat16)
    y_glob = lax.dynamic_slice_in_dim(
        layer_out[:, block_len:], half_index * glob_half, glob_half, 1
    ).astype(jnp.bfloat16)
    grad_long, grad_glob = (
        lax.all_gather(dy_long, "ffn", axis=1, tiled=True),
        lax.all_gather(dy_glob, "ffn", axis=1, tiled=True),
    )
    grad_rows = jnp.concatenate([grad_long, grad_glob], axis=1).astype(jnp.float32)
    norm_two_val, norm_two_back = jax.vjp(layer_norm, pre_out, norm_params[2], norm_params[3])
    d_pre, d_gain_two, d_bias_two = norm_two_back(grad_rows)
    d_pre_low = d_pre.astype(jnp.bfloat16)
    grad_down = jnp.einsum("snf,snd->fd", act_low, d_pre_low, preferred_element_type=jnp.float32)
    d_act = jnp.einsum("snd,fd->snf", d_pre_low, w_down, preferred_element_type=jnp.float32)
    d_up = gelu_back(d_act)[0].astype(jnp.bfloat16)
    grad_up = jnp.einsum("snd,snf->df", norm_low, d_up, preferred_element_type=jnp.float32)
    d_norm_part = jnp.einsum("snf,df->snd", d_up, w_up, preferred_element_type=jnp.float32)
    d_norm_one = lax.psum(d_norm_part, "ffn") + d_pre
    norm_one_val, norm_one_back = jax.vjp(layer_norm, mid_rows, norm_params[0], norm_params[1])
    d_mid, d_gain_one, d_bias_one = norm_one_back(d_norm_one)
    d_mid_low = d_mid.astype(jnp.bfloat16)
    norm_grad = jnp.stack([d_gain_one, d_bias_one, d_gain_two, d_bias_two])
    add_long = lax.dynamic_slice_in_dim(d_mid[:, :block_len], half_index * tok_half, tok_half, 1)
    add_glob = lax.dynamic_slice_in_dim(d_mid[:, block_len:], half_index * glob_half, glob_half, 1)
    grad_out = jnp.einsum("snc,snd->cd", out_rows, d_mid_low, preferred_element_type=jnp.float32)
    d_out_rows = jnp.einsum(
        "snd,cd->snc", d_mid_low, w_out, preferred_element_type=jnp.float32
    ).astype(jnp.bfloat16)
    back_in = attention_inputs(*project_keys(all_rows))
    back_pieces = back_in + (
        sent_mask,
        lse_long,
        lse_glob,
        split_heads(d_out_rows[:, :block_len]),
        split_heads(d_out_rows[:, block_len:]),
    )
    back_out = lax.map(attend_back, tuple((grouped(member) for member in back_pieces)))
    dq_long, dq_glob, dk_ext, dv_ext, dk_loc, dv_loc, dk_all, dv_all = tuple(
        (ungrouped(member) for member in back_out[:8])
    )
    rel_grad = jnp.sum(back_out[8], axis=0).reshape(labels, head_local)
    dkv_ext = jnp.concatenate([merge_heads(dk_ext), merge_heads(dv_ext)], axis=-1)
    dkv_all = jnp.concatenate([merge_heads(dk_all), merge_heads(dv_all)], axis=-1)
    dkv_glob = lax.psum_scatter(dkv_all, "seq", scatter_dimension=1, tiled=True)
    rim_rows = jnp.concatenate([dkv_ext[:, :RADIUS], dkv_ext[:, RADIUS + block_len :]], axis=1)
    rim_back = with_halo(rim_rows.astype(jnp.bfloat16), (("seq", 1),), RADIUS).astype(
        rim_rows.dtype
    )
    dkv_long = dkv_ext[:, RADIUS : RADIUS + block_len] + jnp.concatenate(
        [merge_heads(dk_loc), merge_heads(dv_loc)], axis=-1
    )
    dkv_long = dkv_long.at[:, :RADIUS].add(rim_back[:, :RADIUS])
    dkv_long = dkv_long.at[:, block_len - RADIUS :].add(rim_back[:, 3 * RADIUS :])
    d_proj = jnp.concatenate(
        [
            jnp.concatenate([merge_heads(dq_long), dkv_long], axis=-1),
            jnp.concatenate([merge_heads(dq_glob), dkv_glob], axis=-1),
        ],
        axis=1,
    ).astype(jnp.bfloat16)
    grad_qkv = jnp.einsum("snd,snc->dc", all_rows, d_proj, preferred_element_type=jnp.float32)
    d_in = jnp.einsum("snc,dc->snd", d_proj, w_qkv, preferred_element_type=jnp.float32)
    dx_long, dx_glob = (
        lax.psum_scatter(
            d_in[:, :block_len].astype(jnp.bfloat16), "ffn", scatter_dimension=1, tiled=True
        ).astype(jnp.float32),
        lax.psum_scatter(
            d_in[:, block_len:].astype(jnp.bfloat16), "ffn", scatter_dimension=1, tiled=True
        ).astype(jnp.float32),
    )
    dx_long = dx_long + add_long
    dx_glob = dx_glob + add_glob
    tile_rows = jnp.concatenate(
        [
            cut_tiles(grad_qkv[:, part_idx * head_local : (part_idx + 1) * head_local], side_len)
            for part_idx in range(3)
        ]
        + [
            cut_tiles(grad_out, side_len),
            cut_tiles(grad_up, side_len),
            cut_tiles(grad_down, side_len),
        ],
        axis=0,
    )
    slot_grads = (
        jnp.zeros((slot_count, side_len, side_len), jnp.float32).at[owner_used].set(tile_rows)
    )
    owned_grads = lax.psum_scatter(slot_grads, "seq", scatter_dimension=0, tiled=True)
    rel_sum, norm_sum = lax.psum((rel_grad, norm_grad), "seq")
    w_new, m_new, v_new, left_q, right_q, left_s, right_s = soap_update(
        owned_grads, w_master, m_old, v_old, left_basis, right_basis, left_stats, right_stats
    )
    rel_new, rel_m_new, rel_v_new = adam_update(rel_sum, rel_table, rel_m, rel_v, WEIGHT_DECAY)
    norm_new, norm_m_new, norm_v_new = adam_update(norm_sum, norm_params, norm_m, norm_v, 0.0)
    return (
        y_long,
        y_glob,
        dx_long,
        dx_glob,
        w_new,
        m_new,
        v_new,
        left_q,
        right_q,
        left_s,
        right_s,
        rel_new,
        rel_m_new,
        rel_v_new,
        norm_new,
        norm_m_new,
        norm_v_new,
    )


def solution(mesh):
    in_specs = (
        P(None, ("seq", "ffn"), None),
        P(None, ("seq", "ffn"), None),
        P(None, "seq", None),
        P(None, ("seq", "ffn"), None),
        P(None, ("seq", "ffn"), None),
        P(),
        P(("seq", "ffn"), None, None),
        P(("seq", "ffn"), None, None),
        P(("seq", "ffn"), None, None),
        P(("seq", "ffn"), None, None),
        P(("seq", "ffn"), None, None),
        P(("seq", "ffn"), None, None),
        P(("seq", "ffn"), None, None),
        P(None, "ffn"),
        P(None, "ffn"),
        P(None, "ffn"),
        P(),
        P(),
        P(),
    )
    out_specs = (
        P(None, ("seq", "ffn"), None),
        P(None, ("seq", "ffn"), None),
        P(None, ("seq", "ffn"), None),
        P(None, ("seq", "ffn"), None),
        P(("seq", "ffn"), None, None),
        P(("seq", "ffn"), None, None),
        P(("seq", "ffn"), None, None),
        P(("seq", "ffn"), None, None),
        P(("seq", "ffn"), None, None),
        P(("seq", "ffn"), None, None),
        P(("seq", "ffn"), None, None),
        P(None, "ffn"),
        P(None, "ffn"),
        P(None, "ffn"),
        P(),
        P(),
        P(),
    )
    return jax.shard_map(
        on_device, mesh=mesh, in_specs=in_specs, out_specs=out_specs, check_vma=False
    )
```

profile of v0, /device:TPU:17, one launch (start us, length us, event | category | flops | bytes accessed | tf_op | source)
XLA Modules:
  0.0 1616.9 jit_solution(13710275203341435712)
XLA Ops:
  16.5 98.1 %all-gather.2.cloned.1.call-done = bf16[224,128,128]{2,1,0:T(8,128)(2,1)} async-done(((bf16[14,128,128]{2,1,0:T(8,128)(2,1)}), bf16[224,128,128]{2,1,0:T(8,128)(2,1)}) %all-gather.2.cloned.1.call-update) | async-done | bytes 7340048 | tf_op jit(solution)/shard_map/all_gather | solution.py:233
  114.6 11.4 gather_fusion
  126.0 3.7 broadcast_select_fusion
  129.8 2.8 copy-done.7
  146.6 2.7 convolution_convert_fusion
  153.2 23.6 %all_gather.22 = bf16[2,64,768]{2,0,1:T(2,128)(2,1)S(1)} all-gather(bf16[2,4,768]{2,0,1:T(2,128)(2,1)S(1)} %copy.329), channel_id=1, replica_groups=mesh['seq'=16,'ffn'=2] {'seq'}, dimensions={1}, use_global_device_ids=true | all-gather | bytes 208896 | tf_op jit(solution)/shard_map/all_gather | solution.py:281
  181.3 4.9 collective-permute-start.1
  189.9 5.5 pad.21.clone
  195.4 10.7 reshape.412
  206.1 5.1 slice.261
  211.2 11.2 reshape.413
  222.5 6.3 copy.328
  236.7 3.9 fusion.134
  244.1 3.0 fusion.70
  247.4 5.1 fusion.126
  252.6 3.5 copy.476
  256.0 6.0 reshape.463
  262.0 4.9 copy.477
  266.9 5.5 reshape.462
  272.4 7.7 all-reduce.12.cloned.1.call-done
  285.8 3.2 fusion.118
  289.7 3.0 all_gather.24
  292.8 4.6 all_gather.23
  297.4 17.1 %all-reduce.14.cloned.1.call-done = f32[2,260,768]{2,1,0:T(8,128)} async-done(((f32[2,260,768]{2,1,0:T(8,128)}), f32[2,260,768]{2,1,0:T(8,128)}) %all-reduce.14.cloned.1.call-update) | async-done | bytes 1597456 | tf_op jit(solution)/shard_map/psum | solution.py:375
  318.9 4.2 fusion.7
  324.3 2.6 fusion.136
  330.0 5.7 convolution_bitcast_fusion.1
  335.7 6.7 reshape.430
  342.4 6.8 copy.373
  349.3 5.2 convolution_bitcast_fusion
  354.5 6.6 reshape.432
  361.1 5.8 copy.374
  366.9 2.8 multiply_reduce_fusion.2
  395.3 4.7 copy.410
  408.8 3.1 copy.351
  417.5 2.8 fusion.23
  420.4 3.0 copy.350
  425.9 3.1 collective-permute-start.2
  429.0 4.2 collective-permute-start.3
  435.2 10.3 reshape.420
  445.6 5.2 pad.23
  450.8 8.4 reshape.421
  459.2 2.7 slice.274
  461.9 2.6 copy.408
  473.4 58.9 %all-reduce.19 = (bf16[2,64,768]{2,1,0:T(8,128)(2,1)}, f32[4,768]{1,0:T(4,128)S(1)}) all-reduce(f32[2,64,768]{2,1,0:T(8,128)S(1)} %copy-done.54, f32[4,768]{1,0:T(4,128)S(1)} %pad_maximum_fusion.10), channel_id=2, replica_groups=mesh['seq'=16,'ffn'=2] {'seq'}, use_global_device_ids=true, to_apply=%region_23.24.clone | all-reduce | flops 101376 | bytes 614400
  536.9 3.5 scatter-add.6
  557.1 2.7 copy.368
  562.6 2.7 copy.366
  568.3 2.6 constant_dynamic-update-slice_fusion.7
  578.3 2.7 constant_dynamic-update-slice_fusion.2
  581.0 7.0 broadcast_in_dim.170
  588.1 40.9 %scatter_fusion = f32[224,128,128]{2,1,0:T(8,128)} fusion(f32[224,128,128]{2,1,0:T(8,128)} %broadcast_in_dim.170, s32[216]{0:T(256)S(1)} %copy-done.87, f32[216,128,128]{2,1,0:T(8,128)} %constant_dynamic-update-slice_fusion.2), kind=kCustom, calls=%fused_computation.1 | custom fusion | bytes 42468192 | tf_op jit(solution)/shard_map/scatter | solution.py:465
  634.8 16.2 %all-reduce.4 = bf16[2,4,768]{2,1,0:T(4,128)(2,1)S(1)} all-reduce(bf16[2,4,768]{2,1,0:T(4,128)(2,1)S(1)} %slice.284), channel_id=4, replica_groups=mesh['seq'=16,'ffn'=2] {'ffn'}, use_global_device_ids=true, to_apply=%region_25.26.clone | all-reduce | flops 6144 | bytes 24576
  655.8 296.4 %reduce-scatter.7.cloned.1.call-done = f32[14,128,128]{2,1,0:T(8,128)} async-done(((f32[224,128,128]{2,1,0:T(8,128)}), f32[14,128,128]{2,1,0:T(8,128)}) %reduce-scatter.7.cloned.1.call-update) | async-done | bytes 917520 | tf_op jit(solution)/shard_map/reduce_scatter | solution.py:467
  952.1 3.1 fusion.15
  957.2 2.6 fusion.142
  963.8 2.6 fusion.140
  971.2 165.8 %custom-call.8 = f32[14,128,128]{2,1,0:T(8,128)} custom-call(f32[14,128,128]{2,1,0:T(8,128)} %fusion.40), custom_call_target="Cholesky" | custom-call | tf_op jit(solution)/shard_map/jit(cholesky)/cholesky | solution.py:151
  1141.9 165.6 %custom-call.10 = f32[14,128,128]{2,1,0:T(8,128)} custom-call(f32[14,128,128]{2,1,0:T(8,128)} %fusion.37), custom_call_target="Cholesky" | custom-call | tf_op jit(solution)/shard_map/jit(cholesky)/cholesky | solution.py:151
  1311.0 139.2 %custom-call.11 = f32[14,1,128,128]{2,3,1,0:T(8,128)} custom-call(f32[14,1,128,128]{3,2,1,0:T(8,128)} %get-tuple-element.286), custom_call_target="InvertDiagBlocksLowerTriangular" | custom-call | tf_op jit(solution)/shard_map/triangular_solve/custom-call.0 | solution.py:152
  1450.2 4.0 convolution_bitcast_fusion.5
  1456.6 139.0 %custom-call.9 = f32[14,1,128,128]{2,3,1,0:T(8,128)} custom-call(f32[14,1,128,128]{3,2,1,0:T(8,128)} %get-tuple-element.287), custom_call_target="InvertDiagBlocksLowerTriangular" | custom-call | tf_op jit(solution)/shard_map/triangular_solve/custom-call.0 | solution.py:152
  1595.6 3.7 convolution_bitcast_fusion.6
  1606.7 3.0 fusion.18
  (415 shorter events, 187.2 us)
Async XLA Ops:
  7.2 948.0 %copy-start = (f32[14,128,128]{2,1,0:T(8,128)S(1)}, f32[14,128,128]{2,1,0:T(8,128)}, u32[]{:S(2)}) copy-start(f32[14,128,128]{2,1,0:T(8,128)} %param.36) | copy-start | bytes 2752516
  7.2 5.3 copy-start.92
  7.2 5.9 copy-start.72
  7.3 107.4 %all-gather.2.cloned.1.call-start = ((), (), s32[]{:S(2)}) async-start(), calls=%async_computation.2 | async-start | bytes 7798784 | tf_op jit(solution)/shard_map/all_gather | solution.py:233
  9.5 270.7 %all-reduce.12.cloned.1.call-start = ((), (), s32[]{:S(2)}) async-start(), calls=%async_computation.3 | async-start | bytes 3244032 | tf_op jit(solution)/shard_map/psum | solution.py:367
  15.6 131.0 %copy-start.38 = (bf16[2,260,768]{2,1,0:T(8,128)(2,1)}, bf16[2,260,768]{2,1,0:T(8,128)(2,1)S(1)}, u32[]{:S(2)}) copy-start(bf16[2,260,768]{2,1,0:T(8,128)(2,1)S(1)} %constant_dynamic-update-slice_fusion) | copy-start | bytes 2396164
  129.7 2.8 copy-start.7
  146.6 2.7 copy-start.68
  178.9 57.7 %copy-start.12 = (bf16[2,256,384]{1,2,0:T(8,128)(2,1)}, bf16[2,256,384]{1,2,0:T(8,128)(2,1)S(1)}, u32[]{:S(2)}) copy-start(bf16[2,256,384]{1,2,0:T(8,128)(2,1)S(1)} %copy.323) | copy-start | bytes 1179652
  178.9 50.4 %collective-permute-start = (bf16[2,84,768]{2,1,0:T(8,128)(2,1)}, bf16[2,84,768]{2,1,0:T(8,128)(2,1)}, u32[]{:S(2)}, u32[]{:S(2)}) collective-permute-start(bf16[2,84,768]{2,1,0:T(8,128)(2,1)} %get-tuple-element.280), channel_id=1, source_target_pairs={{0,2},{2,4},{4,6},{6,8},{8,10},{10,12},{12,14},{14,16},{16,18},{18... | collective-permute-start | bytes 774152 | tf_op jit(solution)/shard_map/ppermute | solution.py:33
  181.3 48.0 %collective-permute-start.1 = (bf16[2,84,768]{2,1,0:T(8,128)(2,1)}, bf16[2,84,768]{2,1,0:T(8,128)(2,1)}, u32[]{:S(2)}, u32[]{:S(2)}) collective-permute-start(bf16[2,84,768]{2,1,0:T(8,128)(2,1)} %get-tuple-element.281), channel_id=1, source_target_pairs={{2,0},{4,2},{6,4},{8,6},{10,8},{12,10},{14,12},{16,14},{18,16},{20... | collective-permute-start | bytes 774152 | tf_op jit(solution)/shard_map/ppermute | solution.py:35
  222.5 6.3 copy-start.51
  233.8 2.9 copy-start.58
  236.0 5.8 copy-start.22
  244.1 3.0 copy-start.36
  244.1 3.3 copy-start.75
  247.1 67.4 %all-reduce.14.cloned.1.call-start = ((), (), s32[]{:S(2)}) async-start(), calls=%async_computation.4 | async-start | bytes 3244032 | tf_op jit(solution)/shard_map/psum | solution.py:375
  282.5 3.3 copy-start.45
  289.1 77.9 %all-reduce.16.cloned.1.call-start = ((), (), s32[]{:S(2)}) async-start(), calls=%async_computation.5 | async-start | bytes 3244032 | tf_op jit(solution)/shard_map/psum | solution.py:397
  314.5 3.6 copy-start.96
  318.9 5.4 copy-start.48
  326.9 324.7 %all-reduce.18.cloned.1.call-start = ((), (), s32[]{:S(2)}) async-start(), calls=%async_computation.8 | async-start | bytes 540672 | tf_op jit(solution)/shard_map/psum | solution.py:468
  342.4 6.8 copy-start.5
  342.4 6.8 copy-start.18
  342.4 6.8 copy-start.97
  372.9 11.4 slice-start
  377.3 3.8 copy-start.25
  377.3 5.2 copy-start.9
  377.3 5.2 copy-start.37
  378.4 5.9 slice-start.1
  395.3 4.7 copy-start.79
  395.3 5.3 copy-start.78
  395.3 6.5 copy-start.53
  395.3 7.4 copy-start.55
  400.0 3.9 copy-start.40
  401.9 3.2 copy-start.41
  408.8 8.7 copy-start.3
  420.4 3.0 copy-start.19
  423.4 9.7 copy-start.16
  425.9 108.8 %collective-permute-start.2 = (bf16[2,84,768]{2,1,0:T(8,128)(2,1)}, bf16[2,84,768]{2,1,0:T(8,128)(2,1)}, u32[]{:S(2)}, u32[]{:S(2)}) collective-permute-start(bf16[2,84,768]{2,1,0:T(8,128)(2,1)} %get-tuple-element.276), channel_id=1, source_target_pairs={{0,2},{2,4},{4,6},{6,8},{8,10},{10,12},{12,14},{14,16},{16,18},{18... | collective-permute-start | bytes 774152 | tf_op jit(solution)/shard_map/ppermute | solution.py:33
  429.0 105.7 %collective-permute-start.3 = (bf16[2,84,768]{2,1,0:T(8,128)(2,1)}, bf16[2,84,768]{2,1,0:T(8,128)(2,1)}, u32[]{:S(2)}, u32[]{:S(2)}) collective-permute-start(bf16[2,84,768]{2,1,0:T(8,128)(2,1)} %get-tuple-element.277), channel_id=1, source_target_pairs={{2,0},{4,2},{6,4},{8,6},{10,8},{12,10},{14,12},{16,14},{18,16},{20... | collective-permute-start | bytes 774152 | tf_op jit(solution)/shard_map/ppermute | solution.py:35
  464.5 4.4 copy-start.42
  468.9 4.5 copy-start.80
  468.9 4.5 copy-start.81
  468.9 4.5 copy-start.82
  468.9 4.5 copy-start.83
  468.9 4.5 copy-start.54
  471.3 61.8 %copy-start.44 = (f32[2,256,384]{2,1,0:T(8,128)S(1)}, f32[2,256,384]{2,1,0:T(8,128)}, u32[]{:S(2)}) copy-start(f32[2,256,384]{2,1,0:T(8,128)} %copy.358) | copy-start | bytes 2359300
  473.3 180.4 %reduce-scatter.5.cloned.1.call-start = ((), (), s32[]{:S(2)}) async-start(), calls=%async_computation.6 | async-start | bytes 1179648 | tf_op jit(solution)/shard_map/reduce_scatter | solution.py:443
  548.8 403.3 %reduce-scatter.7.cloned.1.call-start = ((), (), s32[]{:S(2)}) async-start(), calls=%async_computation.7 | async-start | bytes 15597568 | tf_op jit(solution)/shard_map/reduce_scatter | solution.py:467
  565.3 10.4 slice-start.3
  568.3 2.6 copy-start.28
  568.3 7.4 slice-start.4
  574.5 3.6 slice-start.5
  575.7 2.7 slice-start.6
  581.0 7.1 copy-start.87
  632.7 19.0 %copy-start.57 = (f32[169,384]{1,0:T(8,128)S(1)}, f32[169,384]{1,0:T(8,128)}, u32[]{:S(2)}) copy-start(f32[169,384]{1,0:T(8,128)} %param.39) | copy-start | bytes 778756
  632.7 18.9 %copy-start.73 = (f32[169,384]{1,0:T(8,128)S(1)}, f32[169,384]{1,0:T(8,128)}, u32[]{:S(2)}) copy-start(f32[169,384]{1,0:T(8,128)} %param.40) | copy-start | bytes 778756
  632.8 18.9 %copy-start.74 = (f32[169,384]{1,0:T(8,128)S(1)}, f32[169,384]{1,0:T(8,128)}, u32[]{:S(2)}) copy-start(f32[169,384]{1,0:T(8,128)} %param.41) | copy-start | bytes 778756
  632.8 20.9 %slice-start.2 = ((f32[2,260,768]{2,1,0:T(8,128)}), f32[2,256,768]{2,1,0:T(8,128)S(1)}, s32[]{:S(2)}) async-start(f32[2,260,768]{2,1,0:T(8,128)} %copy-done.8), calls=%async_computation.11 | async-start | bytes 3145728 | tf_op jit(solution)/shard_map/slice | solution.py:402
  653.7 298.5 %copy-start.59 = (f32[14,128,128]{2,1,0:T(8,128)S(1)}, f32[14,128,128]{2,1,0:T(8,128)}, u32[]{:S(2)}) copy-start(f32[14,128,128]{2,1,0:T(8,128)} %param.38) | copy-start | bytes 2752516
  955.2 4.6 copy-start.30
  957.2 2.6 copy-start.60
  959.8 3.0 copy-start.34
  (53 other events, 82.5 us)
Sparse Core Ops, SparseCore 0:
  11.4 103.2 all-gather.1
  247.2 32.8 all-reduce.11
  289.2 25.2 all-reduce.13
  327.1 21.6 all-reduce.15
  473.4 104.9 all-reduce.17
  581.1 11.0 reduce-scatter.4
  629.1 322.9 reduce-scatter.6
where the time goes:
time: 1630 us; the launch traced here: 1620 us
  other arithmetic  652 us (40%)
  waiting for transfers between devices  419 us (26%)
  local copies, waits for them, and re-layouts  308 us (19%)
  blocking collectives  111 us (7%)
  matrix products  93.6 us (6%)
  between operations  17.3 us (1%)
    another operation x6, other arithmetic, chol_orth(): lower_f = jnp.linalg.cholesky(gram_mat)  333 us
    reduce_scatter x1, waiting for transfers between devices, on_device(): lax.psum_scatter(slot_grads, 'seq', scatter_dimension=0, tiled=True)  296 us
    another operation x4, other arithmetic, chol_orth(): lax.linalg.triangular_solve(lower_f, jnp.swapaxes(matrix, 1, 2), left_sid...  280 us
    all_gather x1, waiting for transfers between devices, on_device(): lax.all_gather(w_master.astype(jnp.bfloat16), 'seq', axis=0, tiled=True)  98.1 us
    unnamed x2, blocking collectives  75.1 us
    unnamed x230, local copies, waits for them, and re-layouts  50.9 us
    scatter x1, local copies, waits for them, and re-layouts, on_device(): jnp.zeros((slot_count, side_len, side_len), jnp.float32).at[owner_used]  40.9 us
  transfers between devices with their start and end apart: 11, of which 4 were waited for; matrix products, arithmetic and copies ran while one was open for 15% of the time, Pallas kernels for 0%

commit v1 on v0

--- a/solution.py
+++ b/solution.py
@@ -3,6 +3,8 @@
 import jax
 import jax.numpy as jnp
 from jax import lax
+from jax.experimental import pallas as pl
+from jax.experimental.pallas import tpu as pltpu
 from jax.sharding import PartitionSpec as P
 
 HEADS = 12
@@ -142,39 +144,242 @@
     return jnp.einsum(formula, *operands, precision=TOP_PRECISION)
 
 
-def sandwich(left_q, middle, right_q):
-    return einsum_high("nik,nkl->nil", einsum_high("nji,njk->nik", left_q, middle), right_q)
-
-
-def chol_orth(matrix):
-    gram_mat = einsum_high("nji,njk->nik", matrix, matrix)
-    lower_f = jnp.linalg.cholesky(gram_mat)
-    solved = lax.linalg.triangular_solve(
-        lower_f, jnp.swapaxes(matrix, 1, 2), left_side=True, lower=True
-    )
-    return jnp.swapaxes(solved, 1, 2)
-
-
-def soap_update(grad_tile, weight, first_mom, second_mom, left_q, right_q, left_s, right_s):
-    rotated = sandwich(left_q, grad_tile, right_q)
-    first_mom = BETA_ONE * first_mom + (1.0 - BETA_ONE) * rotated
-    second_mom = BETA_TWO * second_mom + (1.0 - BETA_TWO) * rotated * rotated
-    direction = (
-        first_mom
-        / (1.0 - BETA_ONE**STEP)
-        / (jnp.sqrt(second_mom / (1.0 - BETA_TWO**STEP)) + ADAM_EPS)
-    )
-    back_rot = einsum_high("nik,nlk->nil", einsum_high("nij,njk->nik", left_q, direction), right_q)
-    weight = weight - LEARN_RATE * (back_rot + WEIGHT_DECAY * weight)
-    left_s = BETA_TWO * left_s + (1.0 - BETA_TWO) * einsum_high(
-        "nik,njk->nij", grad_tile, grad_tile
-    )
-    right_s = BETA_TWO * right_s + (1.0 - BETA_TWO) * einsum_high(
-        "nki,nkj->nij", grad_tile, grad_tile
-    )
-    left_q = chol_orth(einsum_high("nij,njk->nik", left_s, left_q))
-    right_q = chol_orth(einsum_high("nij,njk->nik", right_s, right_q))
-    return (weight, first_mom, second_mom, left_q, right_q, left_s, right_s)
+def seq_bits(count):
+    return [1 << at for at in range(count.bit_length() - 1)]
+
+
+def swap_with(values, bit):
+    count = lax.axis_size("seq")
+    return lax.ppermute(values, "seq", [(i, i ^ bit) for i in range(count)])
+
+
+def slot_parts(slots, count):
+    bits = seq_bits(count)
+    low, high = bits[:2], bits[2:]
+    half = slots // 2
+    return [(0, half, low + high), (half, slots, low[::-1] + high)]
+
+
+def gather_slots(tiles):
+    gathered = []
+    for first, last, order in slot_parts(tiles.shape[0], lax.axis_size("seq")):
+        cells = tiles[first:last]
+        for bit in order[::-1]:
+            cells = jnp.concatenate([cells, swap_with(cells, bit)], axis=0)
+        gathered.append(cells)
+    return gathered
+
+
+def slot_places(owners, slots):
+    count = lax.axis_size("seq")
+    apart = (owners // slots) ^ lax.axis_index("seq")
+    inner = owners % slots
+    place = jnp.zeros_like(owners)
+    for first, last, order in slot_parts(slots, count):
+        index = jnp.zeros_like(owners)
+        for at, bit in enumerate(order):
+            index = index + jnp.where((apart & bit) != 0, count >> (at + 1), 0)
+        here = (inner >= first) & (inner < last)
+        place = jnp.where(here, first * count + index * (last - first) + inner - first, place)
+    return place
+
+
+def scatter_slots(cells_all, slots):
+    sums = []
+    count = lax.axis_size("seq")
+    for first, last, order in slot_parts(slots, count):
+        cells = cells_all[first * count : last * count]
+        for bit in order:
+            half = cells.shape[0] // 2
+            got = swap_with(cells[half:], bit)
+            cells = cells[:half].astype(jnp.float32) + got.astype(jnp.float32)
+            if bit != order[-1]:
+                cells = cells.astype(jnp.bfloat16)
+        sums.append(cells)
+    return jnp.concatenate(sums, axis=0)
+
+
+BF = jnp.bfloat16
+F32 = jnp.float32
+
+
+def split_two(x):
+    hi = x.astype(BF)
+    return hi, (x - hi.astype(F32)).astype(BF)
+
+
+def split_three(x):
+    hi = x.astype(BF)
+    rest = x - hi.astype(F32)
+    mid = rest.astype(BF)
+    return hi, mid, (rest - mid.astype(F32)).astype(BF)
+
+
+def left_six(parts, axis):
+    h, m, l = parts
+    return jnp.concatenate([h, h, m, m, h, l], axis=axis)
+
+
+def right_six(parts, axis):
+    h, m, l = parts
+    return jnp.concatenate([h, m, h, m, l, h], axis=axis)
+
+
+def left_three(parts, axis):
+    h, l = parts
+    return jnp.concatenate([h, h, l], axis=axis)
+
+
+def right_three(parts, axis):
+    h, l = parts
+    return jnp.concatenate([h, l, h], axis=axis)
+
+
+def dot_on(a, b, ca, cb):
+    return lax.dot_general(a, b, (((ca,), (cb,)), ((), ())), preferred_element_type=F32)
+
+
+def dot_six(a, b, ca, cb):
+    return dot_on(left_six(split_three(a), ca), right_six(split_three(b), cb), ca, cb)
+
+
+def dot_three(a, b, ca, cb):
+    return dot_on(left_three(split_two(a), ca), right_three(split_two(b), cb), ca, cb)
+
+
+PANEL = 32
+
+
+def panel_inverse(a_ref, t_ref, npad, side, at):
+    groups = PANEL // 8
+    iota = lax.broadcasted_iota(jnp.int32, (8, npad), 0)
+    a = []
+    for i in range(PANEL):
+        rows = a_ref[pl.ds(at + i, npad, stride=side), :]
+        cols = rows.T[at : at + PANEL]
+        a.append([cols[8 * g : 8 * g + 8] for g in range(groups)])
+    z = [[None] * groups for _ in range(PANEL)]
+    for j in range(PANEL):
+        gj, sj = divmod(j, 8)
+        r = lax.rsqrt(a[j][gj][sj : sj + 1])
+        u = [None if g < gj else a[j][g] * r for g in range(groups)]
+        below = list(u)
+        below[gj] = jnp.where(iota > sj, u[gj], 0.0)
+        for k in range(j + 1, PANEL):
+            gk, sk = divmod(k, 8)
+            row = u[gk][sk : sk + 1]
+            for g in range(gk, groups):
+                a[k][g] = a[k][g] - u[g] * row
+        for c in range(j):
+            row = z[c][gj][sj : sj + 1] * r
+            z[c][gj] = jnp.where(iota == sj, row, z[c][gj]) - below[gj] * row
+            for g in range(gj + 1, groups):
+                z[c][g] = z[c][g] - u[g] * row
+        z[j] = [
+            jnp.zeros((8, npad), F32)
+            if g < gj
+            else (jnp.where(iota == sj, r, 0.0) - below[g] * r if g == gj else -u[g] * r)
+            for g in range(groups)
+        ]
+    fill = jnp.zeros((side - PANEL, npad), F32)
+    for c in range(PANEL):
+        t_ref[pl.ds(c, npad, stride=PANEL), :] = jnp.concatenate(z[c] + [fill], axis=0).T
+
+
+def soap_kernel(
+    n, npad, g_ref, w_ref, m_ref, v_ref, ql_ref, qr_ref, sl_ref, sr_ref,
+    w_out, m_out, v_out, ql_out, qr_out, sl_out, sr_out, a_ref, y_ref, mat_ref, t_ref,
+):
+    side = g_ref.shape[-1]
+    eye = (
+        lax.broadcasted_iota(jnp.int32, (side, side), 0)
+        == lax.broadcasted_iota(jnp.int32, (side, side), 1)
+    ).astype(F32)
+
+    def first(i, carry):
+        grad = g_ref[i]
+        left, right = ql_ref[i], qr_ref[i]
+        rotated = dot_three(dot_three(left, grad, 0, 0), right, 1, 0)
+        mom = BETA_ONE * m_ref[i] + (1.0 - BETA_ONE) * rotated
+        sec = BETA_TWO * v_ref[i] + (1.0 - BETA_TWO) * rotated * rotated
+        m_out[i] = mom
+        v_out[i] = sec
+        step = (
+            mom / (1.0 - BETA_ONE**STEP) / (jnp.sqrt(sec / (1.0 - BETA_TWO**STEP)) + ADAM_EPS)
+        )
+        back = dot_three(dot_three(left, step, 1, 0), right, 1, 1)
+        w = w_ref[i]
+        w_out[i] = w - LEARN_RATE * (back + WEIGHT_DECAY * w)
+        parts = split_two(grad)
+        new_l = BETA_TWO * sl_ref[i] + (1.0 - BETA_TWO) * dot_on(
+            left_three(parts, 1), right_three(parts, 1), 1, 1
+        )
+        new_r = BETA_TWO * sr_ref[i] + (1.0 - BETA_TWO) * dot_on(
+            left_three(parts, 0), right_three(parts, 0), 0, 0
+        )
+        sl_out[i] = new_l
+        sr_out[i] = new_r
+        for at, stats, basis in ((0, new_l, left), (1, new_r, right)):
+            mat = dot_six(stats, basis, 1, 0)
+            mat_ref[2 * i + at] = mat
+            parts = split_three(mat)
+            gram = dot_on(left_six(parts, 0), right_six(parts, 0), 0, 0)
+            rows = pl.ds(pl.multiple_of((2 * i + at) * side, side), side)
+            a_ref[rows, :] = gram
+            y_ref[rows, :] = eye
+        return carry
+
+    lax.fori_loop(0, n, first, 0)
+    if npad > 2 * n:
+        a_ref[2 * n * side :, :] = jnp.concatenate([eye] * (npad - 2 * n), axis=0)
+    for at in range(0, side, PANEL):
+        panel_inverse(a_ref, t_ref, npad, side, at)
+
+        def update(b, carry):
+            t = t_ref[pl.ds(pl.multiple_of(b * PANEL, PANEL), PANEL), :][:, :PANEL]
+            base = pl.multiple_of(b * side, side)
+            rows = pl.ds(base + at, PANEL)
+            both = jnp.concatenate([a_ref[rows, :], y_ref[rows, :]], axis=1)
+            fresh = dot_six(t, both, 0, 0)
+            y_ref[rows, :] = fresh[:, side:]
+            if at + PANEL < side:
+                parts = split_three(fresh)
+                cut = tuple(p[:, :side] for p in parts)
+                change = dot_on(left_six(cut, 0), right_six(parts, 0), 0, 0)[at + PANEL :]
+                rest = pl.ds(base + at + PANEL, side - at - PANEL)
+                a_ref[rest, :] = a_ref[rest, :] - change[:, :side]
+                y_ref[rest, :] = y_ref[rest, :] - change[:, side:]
+            return carry
+
+        lax.fori_loop(0, 2 * n, update, 0)
+
+    def last(i, carry):
+        for at, out in ((0, ql_out), (1, qr_out)):
+            rows = pl.ds(pl.multiple_of((2 * i + at) * side, side), side)
+            out[i] = dot_three(mat_ref[2 * i + at], y_ref[rows, :], 1, 1)
+        return carry
+
+    lax.fori_loop(0, n, last, 0)
+
+
+def soap_update(grad, *state):
+    n, side = grad.shape[0], grad.shape[1]
+    npad = -(-2 * n // 8) * 8
+    shape = jax.ShapeDtypeStruct((n, side, side), F32)
+    return pl.pallas_call(
+        lambda *refs: soap_kernel(n, npad, *refs),
+        out_shape=(shape,) * 7,
+        in_specs=[pl.BlockSpec(memory_space=pltpu.VMEM)] * 8,
+        out_specs=(pl.BlockSpec(memory_space=pltpu.VMEM),) * 7,
+        scratch_shapes=[
+            pltpu.VMEM((npad * side, side), F32),
+            pltpu.VMEM((npad * side, side), F32),
+            pltpu.VMEM((2 * n, side, side), F32),
+            pltpu.VMEM((npad * PANEL, side), F32),
+        ],
+        compiler_params=pltpu.CompilerParams(vmem_limit_bytes=48 * 2**20),
+        name="soap",
+    )(grad, *state)
 
 
 def adam_update(grad_vals, param, first_mom, second_mom, decay_rate):
@@ -230,8 +435,9 @@
     span_len = block_len + 2 * RADIUS
     group_len = math.gcd(seq_total, 4)
     half_index = lax.axis_index("ffn")
-    gathered = lax.all_gather(w_master.astype(jnp.bfloat16), "seq", axis=0, tiled=True)
-    tile_set = jnp.take(gathered, owner_used, axis=0)
+    places = slot_places(owner_list, w_master.shape[0])
+    gathered = jnp.concatenate(gather_slots(w_master.astype(jnp.bfloat16)), axis=0)
+    tile_set = jnp.take(gathered, places[:tile_count], axis=0)
     w_qkv = jnp.concatenate(
         [
             assemble(
@@ -461,10 +667,11 @@
         ],
         axis=0,
     )
-    slot_grads = (
-        jnp.zeros((slot_count, side_len, side_len), jnp.float32).at[owner_used].set(tile_rows)
-    )
-    owned_grads = lax.psum_scatter(slot_grads, "seq", scatter_dimension=0, tiled=True)
+    held = jnp.zeros((slot_count,), jnp.int32).at[places].set(jnp.arange(slot_count, dtype=jnp.int32))
+    tile_low = jnp.concatenate(
+        [tile_rows.astype(jnp.bfloat16), jnp.zeros((slot_count - tile_count, side_len, side_len), jnp.bfloat16)]
+    )
+    owned_grads = scatter_slots(jnp.take(tile_low, held, axis=0), w_master.shape[0])
     rel_sum, norm_sum = lax.psum((rel_grad, norm_grad), "seq")
     w_new, m_new, v_new, left_q, right_q, left_s, right_s = soap_update(
         owned_grads, w_master, m_old, v_old, left_basis, right_basis, left_stats, right_stats

time: 1630 us -> 836 us (0.51)
  other arithmetic: 652 us -> 59.1 us
  waiting for transfers between devices: 419 us -> 205 us
  Pallas kernels: 0 us -> 70.6 us
  local copies, waits for them, and re-layouts: 308 us -> 238 us
  matrix products: 93.6 us -> 67.2 us
  starting transfers between devices: 15.4 us -> 36.4 us
    another operation x12 -> x2, other arithmetic: 615 us -> 0.24 us  [the longest x6 333 us: chol_orth(): lower_f = jnp.linalg.cholesky(gram_mat)]
    reduce_scatter x1 -> x0, waiting for transfers between devices: 296 us -> none  [on_device(): lax.psum_scatter(slot_grads, 'seq', scatter_dimension=0, tiled=True)]
    ppermute x0 -> x16, waiting for transfers between devices: none -> 105 us  [swap_with(): return lax.ppermute(values, 'seq', [(i, i ^ bit) for i in range(count)])]
    all_gather x1 -> x0, waiting for transfers between devices: 98.1 us -> none  [on_device(): lax.all_gather(w_master.astype(jnp.bfloat16), 'seq', axis=0, tiled=True)]
    pallas_call x0 -> x1, Pallas kernels: none -> 70.6 us  [soap_update(): pl.pallas_call(lambda *refs: soap_kernel(n, npad, *refs), out_shape=(shap...]
    psum x1, waiting for transfers between devices: 0.01 us -> 61.1 us  [on_device(): rel_sum, norm_sum = lax.psum((rel_grad, norm_grad), 'seq')]
    scatter x1, local copies, waits for them, and re-layouts: 40.9 us -> 1.43 us  [on_device(): jnp.zeros((slot_count,), jnp.int32).at[places]]
    ppermute x0 -> x16, starting transfers between devices: none -> 21.1 us  [swap_with(): return lax.ppermute(values, 'seq', [(i, i ^ bit) for i in range(count)])]
  transfers between devices with their start and end apart: 11 -> 25, of which waited for: 4 -> 14; matrix products, arithmetic and copies ran while one was open for 15% -> 22% of each run, Pallas kernels for 0% -> 0%
where the time goes in v1:
time: 836 us; the launch traced here: 819 us
  local copies, waits for them, and re-layouts  238 us (28%)
  waiting for transfers between devices  205 us (25%)
  blocking collectives  126 us (15%)
  Pallas kernels  70.6 us (8%)
  matrix products  67.2 us (8%)
  other arithmetic  59.1 us (7%)
  starting transfers between devices  36.4 us (4%)
  between operations  17.2 us (2%)
    ppermute x16, waiting for transfers between devices, swap_with(): return lax.ppermute(values, 'seq', [(i, i ^ bit) for i in range(count)])  105 us
    unnamed x2, blocking collectives  84.9 us
    pallas_call x1, Pallas kernels, soap_update(): pl.pallas_call(lambda *refs: soap_kernel(n, npad, *refs), out_shape=(shap...  70.6 us
    psum x1, waiting for transfers between devices, on_device(): rel_sum, norm_sum = lax.psum((rel_grad, norm_grad), 'seq')  61.1 us
    unnamed x242, local copies, waits for them, and re-layouts  41.9 us
    all_gather x1, blocking collectives, project_keys(): lax.all_gather(proj_rows[:, block_len:, head_local:], 'seq', axis=1, tile...  24.1 us
    ppermute x16, starting transfers between devices, swap_with(): return lax.ppermute(values, 'seq', [(i, i ^ bit) for i in range(count)])  21.1 us
    psum x1, waiting for transfers between devices, on_device(): attn_full = lax.psum(attn_part, 'ffn')  17.8 us
  transfers between devices with their start and end apart: 25, of which 14 were waited for; matrix products, arithmetic and copies ran while one was open for 22% of the time, Pallas kernels for 0%

profile of v1, /device:TPU:17, one launch (start us, length us, event | category | flops | bytes accessed | tf_op | source)
XLA Modules:
  0.0 819.3 jit_solution(11690891837512664563)
XLA Ops:
  9.3 9.5 %collective-permute-done = bf16[7,128,128]{2,1,0:T(8,128)(2,1)S(1)} collective-permute-done((bf16[7,128,128]{2,1,0:T(8,128)(2,1)S(1)}, bf16[7,128,128]{2,1,0:T(8,128)(2,1)S(1)}, u32[]{:S(2)}, u32[]{:S(2)}) %collective-permute-start) | collective-permute-done | bytes 229408 | tf_op jit(solution)/shard_map/ppermute | solution.py:153
  18.9 5.1 collective-permute-start.1
  24.0 14.3 %collective-permute-done.1 = bf16[14,128,128]{2,1,0:T(8,128)(2,1)S(1)} collective-permute-done((bf16[14,128,128]{2,1,0:T(8,128)(2,1)S(1)}, bf16[14,128,128]{2,1,0:T(8,128)(2,1)S(1)}, u32[]{:S(2)}, u32[]{:S(2)}) %collective-permute-start.1) | collective-permute-done | bytes 458784 | tf_op jit(solution)/shard_map/ppermute | solution.py:153
  43.5 8.6 %collective-permute-done.5 = bf16[14,128,128]{2,1,0:T(8,128)(2,1)S(1)} collective-permute-done((bf16[14,128,128]{2,1,0:T(8,128)(2,1)S(1)}, bf16[14,128,128]{2,1,0:T(8,128)(2,1)S(1)}, u32[]{:S(2)}, u32[]{:S(2)}) %collective-permute-start.5) | collective-permute-done | bytes 458784 | tf_op jit(solution)/shard_map/ppermute | solution.py:153
  54.3 5.8 collective-permute-done.2
  62.7 4.4 all_gather.16
  68.1 4.9 collective-permute-done.6
  76.7 7.7 all_gather.17
  88.9 23.4 %collective-permute-done.3 = bf16[56,128,128]{2,1,0:T(8,128)(2,1)} collective-permute-done((bf16[56,128,128]{2,1,0:T(8,128)(2,1)}, bf16[56,128,128]{2,1,0:T(8,128)(2,1)}, u32[]{:S(2)}, u32[]{:S(2)}) %collective-permute-start.3) | collective-permute-done | bytes 1835040 | tf_op jit(solution)/shard_map/ppermute | solution.py:153
  112.3 3.0 constant_dynamic-update-slice_fusion.7
  119.8 3.0 constant_dynamic-update-slice_fusion.2
  122.7 11.4 %gather_fusion = bf16[216,128,128]{2,1,0:T(8,128)(2,1)} fusion(bf16[224,128,128]{2,1,0:T(8,128)(2,1)} %constant_dynamic-update-slice_fusion.2, s32[1024]{0:T(1024)S(1)} %pad_clamp_fusion.1), kind=kCustom, calls=%fused_computation | custom fusion | bytes 14156640 | tf_op jit(solution)/shard_map/jit(_take)/gather | solution.py:440
  134.1 3.7 broadcast_select_fusion.1
  137.9 2.8 copy-done.13
  151.7 24.1 %all_gather.18 = bf16[2,64,768]{2,0,1:T(2,128)(2,1)S(1)} all-gather(bf16[2,4,768]{2,0,1:T(2,128)(2,1)S(1)} %copy.158), channel_id=1, replica_groups=mesh['seq'=16,'ffn'=2] {'seq'}, dimensions={1}, use_global_device_ids=true | all-gather | bytes 208896 | tf_op jit(solution)/shard_map/all_gather | solution.py:487
  179.2 5.3 collective-permute-start.9
  187.4 5.5 pad.22.clone
  192.8 10.8 %reshape.417 = f32[2,6,108800]{2,0,1:T(2,128)} reshape(f32[2,6,256,425]{3,2,0,1:T(8,128)} %pad.22.clone) | data formatting | bytes 10444800 | tf_op jit(solution)/shard_map/while/body/eval_jaxpr/reshape | solution.py:60
  203.6 5.1 slice.340
  208.7 11.2 %reshape.418 = f32[2,6,256,424]{3,2,0,1:T(8,128)} reshape(f32[2,6,108544]{2,0,1:T(2,128)} %slice.340) | data formatting | bytes 10420224 | tf_op jit(solution)/shard_map/while/body/eval_jaxpr/reshape | solution.py:61
  219.9 6.2 copy.157
  235.9 3.7 fusion.117
  246.1 5.1 fusion.108
  253.0 3.7 reshape.471
  256.7 3.3 copy.280
  260.0 2.9 reshape.470
  262.9 17.8 %all-reduce.13.cloned.1.call-done = f32[2,260,768]{2,1,0:T(8,128)} async-done(((f32[2,260,768]{2,1,0:T(8,128)}), f32[2,260,768]{2,1,0:T(8,128)}) %all-reduce.13.cloned.1.call-update) | async-done | bytes 1597456 | tf_op jit(solution)/shard_map/psum | solution.py:573
  286.4 3.2 fusion.99
  293.1 2.7 all_gather.19
  295.8 15.7 %all-reduce.15.cloned.1.call-done = f32[2,260,768]{2,1,0:T(8,128)} async-done(((f32[2,260,768]{2,1,0:T(8,128)}), f32[2,260,768]{2,1,0:T(8,128)}) %all-reduce.15.cloned.1.call-update) | async-done | bytes 1597456 | tf_op jit(solution)/shard_map/psum | solution.py:581
  315.8 4.2 fusion.8
  327.4 5.0 bitcast_convert_fusion.1
  332.5 5.5 reshape.435
  338.0 4.1 copy.202
  342.0 4.5 bitcast_convert_fusion
  346.5 6.0 reshape.437
  352.5 4.0 copy.203
  356.5 2.8 multiply_reduce_fusion.2
  373.6 4.6 fusion.32
  387.2 4.6 copy.213
  399.0 3.1 copy.180
  406.1 2.8 fusion.21
  411.1 3.2 collective-permute-start.10
  414.3 4.2 collective-permute-start.11
  420.6 10.3 %reshape.425 = bf16[2,6,108800]{2,0,1:T(2,128)(2,1)} reshape(bf16[2,6,256,425]{3,2,0,1:T(8,128)(2,1)} %pad.23.clone) | data formatting | bytes 5222400 | tf_op jit(solution)/shard_map/while/body/eval_jaxpr/reshape | solution.py:68
  430.9 5.3 pad.24
  436.2 8.4 %reshape.426 = bf16[2,6,256,426]{3,2,0,1:T(8,128)(2,1)} reshape(bf16[2,6,109056]{2,0,1:T(2,128)(2,1)} %pad.24) | data formatting | bytes 5234688 | tf_op jit(solution)/shard_map/while/body/eval_jaxpr/reshape | solution.py:70
  444.6 2.7 slice.353
  455.7 57.0 %all-reduce.20 = (bf16[2,64,768]{2,1,0:T(8,128)(2,1)}, f32[4,768]{1,0:T(4,128)}) all-reduce(f32[2,64,768]{2,1,0:T(8,128)} %pad_maximum_fusion.11, f32[4,768]{1,0:T(4,128)} %pad_maximum_fusion.17), channel_id=2, replica_groups=mesh['seq'=16,'ffn'=2] {'seq'}, use_global_device_ids=true, to_apply=%region_23.24.clone | all-reduce | flops 101376 | bytes 614400
  517.8 3.5 scatter-add.6
  523.4 3.9 scatter-add.9
  543.2 6.1 concatenate.103
  549.3 11.8 %gather_fusion.1 = bf16[224,128,128]{2,1,0:T(8,128)(2,1)} fusion(bf16[224,128,128]{2,1,0:T(8,128)(2,1)} %concatenate.103, s32[1024]{0:T(1024)} %pad_clamp_fusion), kind=kCustom, calls=%fused_computation.1 | custom fusion | bytes 14680960 | tf_op jit(solution)/shard_map/jit(_take)/gather | solution.py:674
  561.1 3.8 broadcast_select_fusion
  574.7 2.7 convolution_convert_fusion.1
  579.3 16.9 %collective-permute-done.12 = bf16[56,128,128]{2,1,0:T(8,128)(2,1)} collective-permute-done((bf16[56,128,128]{2,1,0:T(8,128)(2,1)}, bf16[56,128,128]{2,1,0:T(8,128)(2,1)}, u32[]{:S(2)}, u32[]{:S(2)}) %collective-permute-start.12) | collective-permute-done | bytes 1835040 | tf_op jit(solution)/shard_map/ppermute | solution.py:153
  597.8 5.0 add_convert_fusion.1
  610.7 27.9 %all-reduce.5 = bf16[2,4,768]{2,1,0:T(4,128)(2,1)S(1)} all-reduce(bf16[2,4,768]{2,1,0:T(4,128)(2,1)S(1)} %slice.363), channel_id=4, replica_groups=mesh['seq'=16,'ffn'=2] {'ffn'}, use_global_device_ids=true, to_apply=%region_25.26.clone | all-reduce | flops 6144 | bytes 24576
  639.2 61.1 %all-reduce.19.cloned.1.call-done = f32[169,384]{1,0:T(8,128)} async-done(((f32[169,384]{1,0:T(8,128)}), f32[169,384]{1,0:T(8,128)}) %all-reduce.19.cloned.1.call-update) | async-done | bytes 259600 | tf_op jit(solution)/shard_map/psum | solution.py:675
  709.1 5.0 reduce-scatter.4.cloned.1.call-done
  717.3 8.1 collective-permute-done.14
  726.7 2.8 collective-permute-start.15
  729.5 12.0 %collective-permute-done.15 = bf16[7,128,128]{2,1,0:T(8,128)(2,1)S(1)} collective-permute-done((bf16[7,128,128]{2,1,0:T(8,128)(2,1)S(1)}, bf16[7,128,128]{2,1,0:T(8,128)(2,1)S(1)}, u32[]{:S(2)}, u32[]{:S(2)}) %collective-permute-start.15) | collective-permute-done | bytes 229408 | tf_op jit(solution)/shard_map/ppermute | solution.py:153
  741.7 70.6 %soap.1 = (f32[14,128,128]{2,1,0:T(8,128)}, f32[14,128,128]{2,1,0:T(8,128)}, f32[14,128,128]{2,1,0:T(8,128)}, f32[14,128,128]{2,1,0:T(8,128)}, f32[14,128,128]{2...) custom-call(f32[14,128,128]{2,1,0:T(8,128)S(1)} %pad_maximum_fusion.6.refs_0_, ...), custom_call_target="tpu_custom_call" | custom-call | tf_op jit(solution)/shard_map/soap/pallas_call | solution.py:369
  (456 shorter events, 185.0 us)
Async XLA Ops:
  7.2 273.5 %all-reduce.13.cloned.1.call-start = ((), (), s32[]{:S(2)}) async-start(), calls=%async_computation.1 | async-start | bytes 3244032 | tf_op jit(solution)/shard_map/psum | solution.py:573
  8.5 15.5 %copy-start.45 = (bf16[14,128,128]{2,1,0:T(8,128)(2,1)}, bf16[14,128,128]{2,1,0:T(8,128)(2,1)S(1)}, u32[]{:S(2)}) copy-start(bf16[14,128,128]{2,1,0:T(8,128)(2,1)S(1)} %convert_element_type.185) | copy-start | bytes 1376260
  9.3 33.5 %copy-start.98 = (s32[224]{0:T(256)S(1)}, s32[224]{0:T(256)}, u32[]{:S(2)}) copy-start(s32[224]{0:T(256)} %param.28) | copy-start | bytes 2692
  9.3 9.5 %collective-permute-start = (bf16[7,128,128]{2,1,0:T(8,128)(2,1)S(1)}, bf16[7,128,128]{2,1,0:T(8,128)(2,1)S(1)}, u32[]{:S(2)}, u32[]{:S(2)}) collective-permute-start(bf16[7,128,128]{2,1,0:T(8,128)(2,1)S(1)} %get-tuple-element.215), channel_id=1, source_target_pairs={{0,16},{2,18},{4,20},{6,22},{8,24},{10,26},{12,28},{14,30},{16,0},... | collective-permute-start | bytes 688136 | tf_op jit(solution)/shard_map/ppermute | solution.py:153
  18.9 19.4 %collective-permute-start.1 = (bf16[14,128,128]{2,1,0:T(8,128)(2,1)S(1)}, bf16[14,128,128]{2,1,0:T(8,128)(2,1)S(1)}, u32[]{:S(2)}, u32[]{:S(2)}) collective-permute-start(bf16[14,128,128]{2,1,0:T(8,128)(2,1)S(1)} %pad_maximum_fusion.8), channel_id=1, source_target_pairs={{0,8},{2,10},{4,12},{6,14},{8,0},{10,2},{12,4},{14,6},{16,24},{18,... | collective-permute-start | bytes 1376264 | tf_op jit(solution)/shard_map/ppermute | solution.py:153
  24.0 16.6 %collective-permute-start.4 = (bf16[7,128,128]{2,1,0:T(8,128)(2,1)S(1)}, bf16[7,128,128]{2,1,0:T(8,128)(2,1)S(1)}, u32[]{:S(2)}, u32[]{:S(2)}) collective-permute-start(bf16[7,128,128]{2,1,0:T(8,128)(2,1)S(1)} %get-tuple-element.213), channel_id=1, source_target_pairs={{0,16},{2,18},{4,20},{6,22},{8,24},{10,26},{12,28},{14,30},{16,0},... | collective-permute-start | bytes 688136 | tf_op jit(solution)/shard_map/ppermute | solution.py:153
  39.3 20.8 %collective-permute-start.2 = (bf16[28,128,128]{2,1,0:T(8,128)(2,1)}, bf16[28,128,128]{2,1,0:T(8,128)(2,1)S(1)}, u32[]{:S(2)}, u32[]{:S(2)}) collective-permute-start(bf16[28,128,128]{2,1,0:T(8,128)(2,1)} %pad_maximum_fusion.4), channel_id=1, source_target_pairs={{0,4},{2,6},{4,0},{6,2},{8,12},{10,14},{12,8},{14,10},{16,20},{18,... | collective-permute-start | bytes 2752520 | tf_op jit(solution)/shard_map/ppermute | solution.py:153
  40.6 11.5 %collective-permute-start.5 = (bf16[14,128,128]{2,1,0:T(8,128)(2,1)S(1)}, bf16[14,128,128]{2,1,0:T(8,128)(2,1)S(1)}, u32[]{:S(2)}, u32[]{:S(2)}) collective-permute-start(bf16[14,128,128]{2,1,0:T(8,128)(2,1)S(1)} %pad_maximum_fusion.9), channel_id=1, source_target_pairs={{0,8},{2,10},{4,12},{6,14},{8,0},{10,2},{12,4},{14,6},{16,24},{18,... | collective-permute-start | bytes 1376264 | tf_op jit(solution)/shard_map/ppermute | solution.py:153
  53.1 19.9 %collective-permute-start.6 = (bf16[28,128,128]{2,1,0:T(8,128)(2,1)}, bf16[28,128,128]{2,1,0:T(8,128)(2,1)}, u32[]{:S(2)}, u32[]{:S(2)}) collective-permute-start(bf16[28,128,128]{2,1,0:T(8,128)(2,1)} %pad_maximum_fusion.5), channel_id=1, source_target_pairs={{0,2},{2,0},{4,6},{6,4},{8,10},{10,8},{12,14},{14,12},{16,18},{18,... | collective-permute-start | bytes 2752520 | tf_op jit(solution)/shard_map/ppermute | solution.py:153
  54.3 8.4 %copy-start.70 = (bf16[2,128,768]{2,1,0:T(8,128)(2,1)S(1)}, bf16[2,128,768]{2,1,0:T(8,128)(2,1)}, u32[]{:S(2)}) copy-start(bf16[2,128,768]{2,1,0:T(8,128)(2,1)} %param.23) | copy-start | bytes 1179652
  61.5 50.8 %collective-permute-start.3 = (bf16[56,128,128]{2,1,0:T(8,128)(2,1)}, bf16[56,128,128]{2,1,0:T(8,128)(2,1)}, u32[]{:S(2)}, u32[]{:S(2)}) collective-permute-start(bf16[56,128,128]{2,1,0:T(8,128)(2,1)} %pad_maximum_fusion.1), channel_id=1, source_target_pairs={{0,2},{2,0},{4,6},{6,4},{8,10},{10,8},{12,14},{14,12},{16,18},{18,... | collective-permute-start | bytes 5505032 | tf_op jit(solution)/shard_map/ppermute | solution.py:153
  68.1 7.7 copy-start.96
  68.1 7.7 copy-start.93
  68.1 7.7 copy-start.59
  75.6 44.2 %collective-permute-start.7 = (bf16[56,128,128]{2,1,0:T(8,128)(2,1)}, bf16[56,128,128]{2,1,0:T(8,128)(2,1)}, u32[]{:S(2)}, u32[]{:S(2)}) collective-permute-start(bf16[56,128,128]{2,1,0:T(8,128)(2,1)} %pad_maximum_fusion.2), channel_id=1, source_target_pairs={{0,4},{2,6},{4,0},{6,2},{8,12},{10,14},{12,8},{14,10},{16,20},{18,... | collective-permute-start | bytes 5505032 | tf_op jit(solution)/shard_map/ppermute | solution.py:153
  88.9 26.4 %copy-start.46 = (bf16[14,128,128]{2,1,0:T(8,128)(2,1)S(1)}, bf16[14,128,128]{2,1,0:T(8,128)(2,1)}, u32[]{:S(2)}) copy-start(bf16[14,128,128]{2,1,0:T(8,128)(2,1)} %copy-done.45) | copy-start | bytes 1376260
  150.1 34.5 %copy-start.52 = (bf16[169,384]{0,1:T(8,128)(2,1)S(1)}, bf16[169,384]{0,1:T(8,128)(2,1)}, u32[]{:S(2)}) copy-start(bf16[169,384]{0,1:T(8,128)(2,1)} %copy.154) | copy-start | bytes 389380
  151.7 78.6 %copy-start.72 = (bf16[2,4,6,64]{3,2,1,0:T(8,128)(2,1)}, bf16[2,4,6,64]{3,2,1,0:T(8,128)(2,1)S(1)}, u32[]{:S(2)}) copy-start(bf16[2,4,6,64]{3,2,1,0:T(8,128)(2,1)S(1)} %squeeze.64) | copy-start | bytes 18436
  177.1 49.0 %copy-start.56 = (bf16[2,64,6,64]{3,2,0,1:T(8,128)(2,1)}, bf16[2,64,6,64]{3,2,0,1:T(8,128)(2,1)S(1)}, u32[]{:S(2)}) copy-start(bf16[2,64,6,64]{3,2,0,1:T(8,128)(2,1)S(1)} %reshape.490) | copy-start | bytes 294916
  177.3 58.6 %copy-start.14 = (bf16[2,256,384]{1,2,0:T(8,128)(2,1)}, bf16[2,256,384]{1,2,0:T(8,128)(2,1)S(1)}, u32[]{:S(2)}) copy-start(bf16[2,256,384]{1,2,0:T(8,128)(2,1)S(1)} %copy.152) | copy-start | bytes 1179652
  177.3 50.9 %collective-permute-start.8 = (bf16[2,84,768]{2,1,0:T(8,128)(2,1)}, bf16[2,84,768]{2,1,0:T(8,128)(2,1)}, u32[]{:S(2)}, u32[]{:S(2)}) collective-permute-start(bf16[2,84,768]{2,1,0:T(8,128)(2,1)} %get-tuple-element.211), channel_id=1, source_target_pairs={{0,2},{2,4},{4,6},{6,8},{8,10},{10,12},{12,14},{14,16},{16,18},{18... | collective-permute-start | bytes 774152 | tf_op jit(solution)/shard_map/ppermute | solution.py:35
  179.2 48.9 %collective-permute-start.9 = (bf16[2,84,768]{2,1,0:T(8,128)(2,1)}, bf16[2,84,768]{2,1,0:T(8,128)(2,1)}, u32[]{:S(2)}, u32[]{:S(2)}) collective-permute-start(bf16[2,84,768]{2,1,0:T(8,128)(2,1)} %get-tuple-element.212), channel_id=1, source_target_pairs={{2,0},{4,2},{6,4},{8,6},{10,8},{12,10},{14,12},{16,14},{18,16},{20... | collective-permute-start | bytes 774152 | tf_op jit(solution)/shard_map/ppermute | solution.py:37
  228.2 12.3 %copy-start.11 = (f32[2,6,256,64]{2,3,1,0:T(8,128)}, f32[2,6,256,64]{2,3,1,0:T(8,128)S(1)}, u32[]{:S(2)}) copy-start(f32[2,6,256,64]{2,3,1,0:T(8,128)S(1)} %get-tuple-element.227) | copy-start | bytes 2359300
  230.2 9.4 %copy-start.32 = (bf16[2,424,384]{1,2,0:T(8,128)(2,1)}, bf16[2,424,384]{1,2,0:T(8,128)(2,1)S(1)}, u32[]{:S(2)}) copy-start(bf16[2,424,384]{1,2,0:T(8,128)(2,1)S(1)} %copy.153) | copy-start | bytes 1953796
  230.2 5.6 copy-start.60
  232.7 8.6 %copy-start.29 = (bf16[2,424,384]{1,2,0:T(8,128)(2,1)}, bf16[2,424,384]{1,2,0:T(8,128)(2,1)S(1)}, u32[]{:S(2)}) copy-start(bf16[2,424,384]{1,2,0:T(8,128)(2,1)S(1)} %copy.151) | copy-start | bytes 1953796
  235.9 7.3 copy-start.81
  245.0 66.5 %all-reduce.15.cloned.1.call-start = ((), (), s32[]{:S(2)}) async-start(), calls=%async_computation.2 | async-start | bytes 3244032 | tf_op jit(solution)/shard_map/psum | solution.py:581
  289.7 66.8 %all-reduce.17.cloned.1.call-start = ((), (), s32[]{:S(2)}) async-start(), calls=%async_computation.3 | async-start | bytes 3244032 | tf_op jit(solution)/shard_map/psum | solution.py:603
  313.6 42.9 %copy-start.8 = (f32[2,260,768]{2,1,0:T(8,128)}, f32[2,260,768]{2,1,0:T(8,128)S(1)}, u32[]{:S(2)}) copy-start(f32[2,260,768]{2,1,0:T(8,128)S(1)} %get-tuple-element.191) | copy-start | bytes 4792324
  314.2 42.3 %copy-start.78 = (f32[2,260]{1,0:T(2,128)}, f32[2,260]{1,0:T(2,128)S(1)}, u32[]{:S(2)}) copy-start(f32[2,260]{1,0:T(2,128)S(1)} %get-tuple-element.219) | copy-start | bytes 6244
  315.8 5.4 copy-start.51
  323.9 376.4 %all-reduce.19.cloned.1.call-start = ((), (), s32[]{:S(2)}) async-start(), calls=%async_computation.5 | async-start | bytes 540672 | tf_op jit(solution)/shard_map/psum | solution.py:675
  366.3 12.0 %slice-start = ((s8[5210112]{0:T(1024)(128)(4,1)}), s8[1015808]{0:T(1024)(128)(4,1)S(1)}, s32[]{:S(2)}) async-start(s8[5210112]{0:T(1024)(128)(4,1)} %bitcast.188), calls=%async_computation.6 | async-start | bytes 2031616
  372.1 6.1 slice-start.1
  373.6 4.7 copy-start.31
  387.2 5.2 copy-start.83
  387.2 5.8 copy-start.80
  387.2 6.8 copy-start.66
  399.0 7.0 copy-start.7
  410.9 7.6 copy-start.18
  411.1 104.5 %collective-permute-start.10 = (bf16[2,84,768]{2,1,0:T(8,128)(2,1)S(1)}, bf16[2,84,768]{2,1,0:T(8,128)(2,1)}, u32[]{:S(2)}, u32[]{:S(2)}) collective-permute-start(bf16[2,84,768]{2,1,0:T(8,128)(2,1)S(1)} %get-tuple-element.207), channel_id=1, source_target_pairs={{0,2},{2,4},{4,6},{6,8},{8,10},{10,12},{12,14},{14,16},{16,18},{18... | collective-permute-start | bytes 774152 | tf_op jit(solution)/shard_map/ppermute | solution.py:35
  414.3 101.3 %collective-permute-start.11 = (bf16[2,84,768]{2,1,0:T(8,128)(2,1)S(1)}, bf16[2,84,768]{2,1,0:T(8,128)(2,1)}, u32[]{:S(2)}, u32[]{:S(2)}) collective-permute-start(bf16[2,84,768]{2,1,0:T(8,128)(2,1)S(1)} %get-tuple-element.208), channel_id=1, source_target_pairs={{2,0},{4,2},{6,4},{8,6},{10,8},{12,10},{14,12},{16,14},{18,16},{20... | collective-permute-start | bytes 774152 | tf_op jit(solution)/shard_map/ppermute | solution.py:37
  549.3 11.8 %copy-start.99 = (pred[224]{0:T(512)(128)(4,1)S(1)}, pred[224]{0:T(512)(128)(4,1)}, u32[]{:S(2)}) copy-start(pred[224]{0:T(512)(128)(4,1)} %compare_and_fusion) | copy-start | bytes 676
  564.9 7.2 copy-start.100
  564.9 8.4 %copy-start.24 = (bf16[2,6,256,169]{2,3,1,0:T(8,128)(2,1)S(1)}, bf16[2,6,256,169]{2,3,1,0:T(8,128)(2,1)}, u32[]{:S(2)}) copy-start(bf16[2,6,256,169]{2,3,1,0:T(8,128)(2,1)} %copy.211) | copy-start | bytes 3115012
  568.9 5.8 copy-start.63
  568.9 27.2 %collective-permute-start.12 = (bf16[56,128,128]{2,1,0:T(8,128)(2,1)}, bf16[56,128,128]{2,1,0:T(8,128)(2,1)}, u32[]{:S(2)}, u32[]{:S(2)}) collective-permute-start(bf16[56,128,128]{2,1,0:T(8,128)(2,1)} %get-tuple-element.196), channel_id=1, source_target_pairs={{0,2},{2,0},{4,6},{6,4},{8,10},{10,8},{12,14},{14,12},{16,18},{18,... | collective-permute-start | bytes 5505032 | tf_op jit(solution)/shard_map/ppermute | solution.py:153
  569.5 28.3 %collective-permute-start.16 = (bf16[56,128,128]{2,1,0:T(8,128)(2,1)}, bf16[56,128,128]{2,1,0:T(8,128)(2,1)}, u32[]{:S(2)}, u32[]{:S(2)}) collective-permute-start(bf16[56,128,128]{2,1,0:T(8,128)(2,1)} %get-tuple-element.197), channel_id=1, source_target_pairs={{0,4},{2,6},{4,0},{6,2},{8,12},{10,14},{12,8},{14,10},{16,20},{18,... | collective-permute-start | bytes 5505032 | tf_op jit(solution)/shard_map/ppermute | solution.py:153
  574.7 139.4 %reduce-scatter.4.cloned.1.call-start = ((), (), s32[]{:S(2)}) async-start(), calls=%async_computation.4 | async-start | bytes 1179648 | tf_op jit(solution)/shard_map/reduce_scatter | solution.py:649
  603.8 98.8 %collective-permute-start.17 = (bf16[28,128,128]{2,1,0:T(8,128)(2,1)}, bf16[28,128,128]{2,1,0:T(8,128)(2,1)}, u32[]{:S(2)}, u32[]{:S(2)}) collective-permute-start(bf16[28,128,128]{2,1,0:T(8,128)(2,1)} %slice.379), channel_id=1, source_target_pairs={{0,2},{2,0},{4,6},{6,4},{8,10},{10,8},{12,14},{14,12},{16,18},{18,... | collective-permute-start | bytes 2752520 | tf_op jit(solution)/shard_map/ppermute | solution.py:153
  607.4 98.2 %collective-permute-start.13 = (bf16[28,128,128]{2,1,0:T(8,128)(2,1)}, bf16[28,128,128]{2,1,0:T(8,128)(2,1)}, u32[]{:S(2)}, u32[]{:S(2)}) collective-permute-start(bf16[28,128,128]{2,1,0:T(8,128)(2,1)} %slice.371), channel_id=1, source_target_pairs={{0,4},{2,6},{4,0},{6,2},{8,12},{10,14},{12,8},{14,10},{16,20},{18,... | collective-permute-start | bytes 2752520 | tf_op jit(solution)/shard_map/ppermute | solution.py:153
  705.1 9.0 %slice-start.2 = ((f32[2,260,768]{2,1,0:T(8,128)}), f32[2,256,768]{2,1,0:T(8,128)S(1)}, s32[]{:S(2)}) async-start(f32[2,260,768]{2,1,0:T(8,128)} %copy-done.16), calls=%async_computation.8 | async-start | bytes 3145728 | tf_op jit(solution)/shard_map/slice | solution.py:608
  705.1 11.0 %collective-permute-start.18 = (bf16[14,128,128]{2,1,0:T(8,128)(2,1)}, bf16[14,128,128]{2,1,0:T(8,128)(2,1)}, u32[]{:S(2)}, u32[]{:S(2)}) collective-permute-start(bf16[14,128,128]{2,1,0:T(8,128)(2,1)} %slice.381), channel_id=1, source_target_pairs={{0,8},{2,10},{4,12},{6,14},{8,0},{10,2},{12,4},{14,6},{16,24},{18,... | collective-permute-start | bytes 1376264 | tf_op jit(solution)/shard_map/ppermute | solution.py:153
  708.2 17.1 %collective-permute-start.14 = (bf16[14,128,128]{2,1,0:T(8,128)(2,1)}, bf16[14,128,128]{2,1,0:T(8,128)(2,1)}, u32[]{:S(2)}, u32[]{:S(2)}) collective-permute-start(bf16[14,128,128]{2,1,0:T(8,128)(2,1)} %slice.373), channel_id=1, source_target_pairs={{0,8},{2,10},{4,12},{6,14},{8,0},{10,2},{12,4},{14,6},{16,24},{18,... | collective-permute-start | bytes 1376264 | tf_op jit(solution)/shard_map/ppermute | solution.py:153
  709.1 6.9 copy-start.37
  709.1 16.3 %copy-start.39 = (bf16[28,128,128]{2,1,0:T(8,128)(2,1)S(1)}, bf16[28,128,128]{2,1,0:T(8,128)(2,1)}, u32[]{:S(2)}) copy-start(bf16[28,128,128]{2,1,0:T(8,128)(2,1)} %copy-done.38) | copy-start | bytes 2752516
  717.2 12.3 %collective-permute-start.19 = (bf16[7,128,128]{2,1,0:T(8,128)(2,1)S(1)}, bf16[7,128,128]{2,1,0:T(8,128)(2,1)S(1)}, u32[]{:S(2)}, u32[]{:S(2)}) collective-permute-start(bf16[7,128,128]{2,1,0:T(8,128)(2,1)S(1)} %slice.383), channel_id=1, source_target_pairs={{0,16},{2,18},{4,20},{6,22},{8,24},{10,26},{12,28},{14,30},{16,0},... | collective-permute-start | bytes 688136 | tf_op jit(solution)/shard_map/ppermute | solution.py:153
  725.4 16.3 %copy-start.4 = (f32[14,128,128]{2,1,0:T(8,128)S(1)}, f32[14,128,128]{2,1,0:T(8,128)}, u32[]{:S(2)}) copy-start(f32[14,128,128]{2,1,0:T(8,128)} %refs_5_.1) | copy-start | bytes 2752516
  726.6 15.0 %copy-start = (f32[14,128,128]{2,1,0:T(8,128)S(1)}, f32[14,128,128]{2,1,0:T(8,128)}, u32[]{:S(2)}) copy-start(f32[14,128,128]{2,1,0:T(8,128)} %refs_1_.1) | copy-start | bytes 2752516
  726.7 15.0 %copy-start.1 = (f32[14,128,128]{2,1,0:T(8,128)S(1)}, f32[14,128,128]{2,1,0:T(8,128)}, u32[]{:S(2)}) copy-start(f32[14,128,128]{2,1,0:T(8,128)} %refs_2_.1) | copy-start | bytes 2752516
  726.7 15.0 %copy-start.2 = (f32[14,128,128]{2,1,0:T(8,128)S(1)}, f32[14,128,128]{2,1,0:T(8,128)}, u32[]{:S(2)}) copy-start(f32[14,128,128]{2,1,0:T(8,128)} %refs_3_.1) | copy-start | bytes 2752516
  726.7 15.0 %copy-start.3 = (f32[14,128,128]{2,1,0:T(8,128)S(1)}, f32[14,128,128]{2,1,0:T(8,128)}, u32[]{:S(2)}) copy-start(f32[14,128,128]{2,1,0:T(8,128)} %refs_4_.1) | copy-start | bytes 2752516
  726.7 14.8 %collective-permute-start.15 = (bf16[7,128,128]{2,1,0:T(8,128)(2,1)S(1)}, bf16[7,128,128]{2,1,0:T(8,128)(2,1)S(1)}, u32[]{:S(2)}, u32[]{:S(2)}) collective-permute-start(bf16[7,128,128]{2,1,0:T(8,128)(2,1)S(1)} %slice.375), channel_id=1, source_target_pairs={{0,16},{2,18},{4,20},{6,22},{8,24},{10,26},{12,28},{14,30},{16,0},... | collective-permute-start | bytes 688136 | tf_op jit(solution)/shard_map/ppermute | solution.py:153
  (70 other events, 169.0 us)
Sparse Core Ops, SparseCore 0:
  245.1 35.5 all-reduce.12
  289.8 21.6 all-reduce.14
  324.0 21.6 all-reduce.16
  574.8 125.4 all-reduce.18
  703.0 11.0 reduce-scatter.3
